TPU v7x, 32 devices: a whole 2x2x4 slice. The times are simulated.
32 devices in a mesh: rep: 2 (over y), grp: 4 (over z), hid: 4 (over x, core).
Axes of the slice: x: 2, y: 2, z: 4, core: 2. Of those that a mesh axis runs over, the one named last changes fastest.
Arguments:
- tokens: bfloat16 [1024, 2304], P(('rep', 'grp')), parts along dimension 0, may hold values from -6 to 6
- routes: int32 [1024, 2], P(('rep', 'grp')), parts along dimension 0, may hold values from 0 to 3, all different within a row; in each aligned block of 128 rows (0 to 127, 128 to 255, ...) at most 64 rows name the same one
- gates: float32 [1024, 2], P(('rep', 'grp')), parts along dimension 0, may hold values from 0.2 to 1
- grad_out: bfloat16 [1024, 2304], P(('rep', 'grp')), parts along dimension 0, may hold values from -6 to 6
- w_gate: bfloat16 [4, 2304, 6144], P('grp', None, 'hid'), may hold values from -0.125 to 0.125
- w_up: bfloat16 [4, 2304, 6144], P('grp', None, 'hid'), may hold values from -0.125 to 0.125
- w_down: bfloat16 [4, 6144, 2304], P('grp', 'hid'), may hold values from -0.078125 to 0.078125
Outputs:
- mixed: bfloat16 [1024, 2304], P(('rep', 'grp', 'hid')), parts along dimension 0
- grad_tokens: bfloat16 [1024, 2304], P(('rep', 'grp', 'hid')), parts along dimension 0
- grad_gate: bfloat16 [8, 2304, 6144], P(('rep', 'grp'), None, 'hid'), parts along dimension 0
- grad_up: bfloat16 [8, 2304, 6144], P(('rep', 'grp'), None, 'hid'), parts along dimension 0
- grad_down: bfloat16 [8, 6144, 2304], P(('rep', 'grp'), 'hid'), parts along dimension 0
There are 2 independent parts, one for each index of `rep`. A program takes and returns all parts, laid end to end along the dimension named above; an argument that names none is the same for every part. Nothing has to cross between parts.
Inputs may be any that keep to these rules, and one draw needn't show every extreme that they name: `routes`: each row names 2 different experts. In each block of 128 rows no expert is named by more than 64 rows, and some block names one expert exactly 64 times.
All inputs are finite; a program needn't handle non-finite values.
Results may differ from a plain program's by a relative error of at most 0.0058.
Values may be sent and summed in bfloat16 or wider, within the bound.
A program may use at most 128 MiB of HBM per device.

v0:
```python
import jax
import jax.numpy as jnp
from jax import lax
from jax.sharding import PartitionSpec as P


def slot_numbers(route_blocks, expert_count):
    onehot = (route_blocks[..., None] == jnp.arange(expert_count, dtype=jnp.int32)).astype(
        jnp.int32
    )
    earlier = jnp.cumsum(onehot, axis=-2) - onehot
    return jnp.sum(earlier * onehot, axis=-1)


def forward_rows(rows_x, weight_gate, weight_up, weight_down):
    gate_pre = jnp.dot(rows_x, weight_gate, preferred_element_type=jnp.float32)
    up_pre = jnp.dot(rows_x, weight_up, preferred_element_type=jnp.float32)
    sigma_gate = jax.nn.sigmoid(gate_pre)
    silu_gate = gate_pre * sigma_gate
    hidden = (silu_gate * up_pre).astype(jnp.bfloat16)
    expert_out = jnp.dot(hidden, weight_down, preferred_element_type=jnp.float32)
    return (gate_pre, up_pre, sigma_gate, silu_gate, hidden, expert_out)


def backward_rows(rows_x, rows_c, weight_gate, weight_up, weight_down, saved):
    gate_pre, up_pre, sigma_gate, silu_gate, hidden, expert_out = saved
    grad_hidden = jnp.dot(rows_c, weight_down.T, preferred_element_type=jnp.float32)
    slope = sigma_gate * (1.0 + gate_pre * (1.0 - sigma_gate))
    grad_pre_gate = (grad_hidden * up_pre * slope).astype(jnp.bfloat16)
    grad_pre_up = (grad_hidden * silu_gate).astype(jnp.bfloat16)
    grad_rows = jnp.dot(grad_pre_gate, weight_gate.T, preferred_element_type=jnp.float32)
    grad_rows = grad_rows + jnp.dot(grad_pre_up, weight_up.T, preferred_element_type=jnp.float32)
    grad_wgate = jnp.dot(rows_x.T, grad_pre_gate, preferred_element_type=jnp.float32).astype(
        jnp.bfloat16
    )
    grad_wup = jnp.dot(rows_x.T, grad_pre_up, preferred_element_type=jnp.float32).astype(
        jnp.bfloat16
    )
    grad_wdown = jnp.dot(hidden.T, rows_c, preferred_element_type=jnp.float32).astype(jnp.bfloat16)
    return (grad_rows, grad_wgate, grad_wup, grad_wdown)


def combine_pairs(whole, weights, row_ids):
    members, groups, capacity, width = whole.shape
    tok_count, top_count = row_ids.shape
    flat = whole.reshape(members, groups * capacity, width)
    picked = jnp.take(flat, row_ids.reshape(-1), axis=1).reshape(
        members, tok_count, top_count, width
    )
    return jnp.sum(weights[..., None] * picked, axis=2)


def send_back(stacked, weights, target_row):
    shares = lax.axis_size("hid")
    share = lax.axis_index("hid")
    tok_rows, top_count = target_row.shape
    summed = lax.psum_scatter(stacked, "hid", scatter_dimension=2, tiled=True)
    moved = lax.all_to_all(summed, "grp", split_axis=1, concat_axis=1, tiled=True)
    whole = lax.all_gather(moved, "hid", axis=2, tiled=True)
    own_count = tok_rows // shares
    own_rows = lax.dynamic_slice_in_dim(target_row, share * own_count, own_count, 0)
    own_weights = lax.dynamic_slice_in_dim(weights, share * own_count, own_count, 1)
    return combine_pairs(whole, own_weights, own_rows)


def local(tokens, routes, gates, grad_out, w_gate, w_up, w_down):
    groups = lax.axis_size("grp")
    shares = lax.axis_size("hid")
    share = lax.axis_index("hid")
    tok_rows, width = tokens.shape
    top_count = routes.shape[1]
    capacity = max(3 * tok_rows // 8, top_count * tok_rows // groups)
    part_slots = capacity // shares
    pairs = tok_rows * top_count
    flat_routes = routes.T.reshape(pairs)
    slot_index = slot_numbers(flat_routes[None, :], groups)[0]
    target_row = flat_routes * capacity + slot_index
    wanted = (
        jnp.arange(groups, dtype=jnp.int32)[:, None] * capacity
        + share * part_slots
        + jnp.arange(part_slots, dtype=jnp.int32)[None, :]
    ).reshape(-1)
    placer = (wanted[:, None] == target_row[None, :]).astype(jnp.bfloat16)
    tok_pairs = jnp.tile(tokens, (top_count, 1))
    cot_pairs = (
        gates.T.reshape(pairs, 1) * jnp.tile(grad_out, (top_count, 1)).astype(jnp.float32)
    ).astype(jnp.bfloat16)
    send_x = (
        jnp.dot(placer, tok_pairs, preferred_element_type=jnp.float32)
        .astype(jnp.bfloat16)
        .reshape(groups, part_slots, width)
    )
    send_c = (
        jnp.dot(placer, cot_pairs, preferred_element_type=jnp.float32)
        .astype(jnp.bfloat16)
        .reshape(groups, part_slots, width)
    )
    arrived = (
        lax.all_to_all(send_x, "grp", split_axis=0, concat_axis=0, tiled=True),
        lax.all_to_all(send_c, "grp", split_axis=0, concat_axis=0, tiled=True),
    )
    block_x, block_c = (
        lax.all_gather(arrived[0], "hid", axis=1, tiled=True),
        lax.all_gather(arrived[1], "hid", axis=1, tiled=True),
    )
    block_shape = block_x.shape
    rows_x = block_x.reshape(-1, width)
    rows_c = block_c.reshape(-1, width)
    weight_gate = w_gate[0]
    weight_up = w_up[0]
    weight_down = w_down[0]
    row_table = target_row.reshape(top_count, tok_rows).T
    plain = jnp.ones_like(gates)
    saved = forward_rows(rows_x, weight_gate, weight_up, weight_down)
    out_terms = saved[5].reshape(block_shape)
    grad_rows, grad_wgate, grad_wup, grad_wdown = backward_rows(
        rows_x, rows_c, weight_gate, weight_up, weight_down, saved
    )
    home_both = send_back(
        jnp.stack([out_terms, grad_rows.reshape(block_shape)]), jnp.stack([gates, plain]), row_table
    )
    home_out = home_both[0]
    home_grad = home_both[1]
    mixed = home_out.astype(jnp.bfloat16)
    grad_tokens = home_grad.astype(jnp.bfloat16)
    return (mixed, grad_tokens, grad_wgate[None], grad_wup[None], grad_wdown[None])


def solution(mesh):
    in_specs = (
        P(("rep", "grp"), None),
        P(("rep", "grp"), None),
        P(("rep", "grp"), None),
        P(("rep", "grp"), None),
        P("grp", None, "hid"),
        P("grp", None, "hid"),
        P("grp", "hid", None),
    )
    out_specs = (
        P(("rep", "grp", "hid"), None),
        P(("rep", "grp", "hid"), None),
        P(("rep", "grp"), None, "hid"),
        P(("rep", "grp"), None, "hid"),
        P(("rep", "grp"), "hid", None),
    )
    return jax.shard_map(local, mesh=mesh, in_specs=in_specs, out_specs=out_specs, check_vma=False)
```

profile of v0, /device:TPU:0, one launch (start us, length us, event | category | flops | bytes accessed | tf_op | source)
XLA Modules:
  0.0 223.7 jit_solution(16238958717698664036)
XLA Ops:
  7.2 0.7 convert_bitcast_fusion
  8.0 1.2 reduce-window.6
  9.8 0.7 fusion.30
  10.5 0.7 multiply_add_fusion
  11.2 1.1 convert_element_type.57
  12.3 0.2 fusion.21
  12.5 0.4 convolution_convert_fusion.3
  12.9 15.8 %all_to_all.15 = bf16[4,16,2304]{2,1,0:T(8,128)(2,1)} all-to-all(bf16[4,16,2304]{2,1,0:T(8,128)(2,1)S(1)} %bitcast.100), channel_id=1, replica_groups=mesh['rep'=2,'grp'=4,'hid'=4] {'grp'}, dimensions={0} | all-to-all | bytes 589824 | tf_op jit(solution)/shard_map/all_to_all | solution.py:100
  28.9 0.4 convolution_convert_fusion.4
  29.2 11.5 %all_to_all.16 = bf16[4,16,2304]{2,1,0:T(8,128)(2,1)} all-to-all(bf16[4,16,2304]{2,1,0:T(8,128)(2,1)S(1)} %bitcast.99), channel_id=1, replica_groups=mesh['rep'=2,'grp'=4,'hid'=4] {'grp'}, dimensions={0} | all-to-all | bytes 589824 | tf_op jit(solution)/shard_map/all_to_all | solution.py:99
  40.8 4.7 %all-gather.6.cloned.1.call-done = bf16[4,64,2304]{2,1,0:T(8,128)(2,1)} async-done(((bf16[4,16,2304]{2,1,0:T(8,128)(2,1)}), bf16[4,64,2304]{2,1,0:T(8,128)(2,1)}) %all-gather.6.cloned.1.call-update) | async-done | bytes 1179664 | tf_op jit(solution)/shard_map/all_gather | solution.py:104
  45.4 6.5 %fusion.5 = f32[256,1536]{1,0:T(8,128)} fusion(bf16[256,2304]{1,0:T(8,128)(2,1)} %bitcast.97, bf16[1,1536,2304]{2,1,0:T(8,128)(2,1)} %param.13), kind=kOutput, calls=%fused_computation.9 | convolution fusion | flops 1811939328 | bytes 9830400 | tf_op jit(solution)/shard_map/dot_general | solution.py:27
  52.0 12.5 %all-gather.4.cloned.1.call-done = bf16[4,64,2304]{2,1,0:T(8,128)(2,1)} async-done(((bf16[4,16,2304]{2,1,0:T(8,128)(2,1)}), bf16[4,64,2304]{2,1,0:T(8,128)(2,1)}) %all-gather.4.cloned.1.call-update) | async-done | bytes 1179664 | tf_op jit(solution)/shard_map/all_gather | solution.py:103
  64.5 5.5 %fusion.13 = f32[256,1536]{1,0:T(8,128)S(1)} fusion(bf16[256,2304]{1,0:T(8,128)(2,1)} %bitcast.89, bf16[1,2304,1536]{2,1,0:T(8,128)(2,1)} %param.11), kind=kOutput, calls=%fused_computation.17 | convolution fusion | flops 1811939328 | bytes 9830400 | tf_op jit(solution)/shard_map/dot_general | solution.py:16
  70.1 5.5 %multiply_convert_fusion.2 = (bf16[256,1536]{1,0:T(8,128)(2,1)S(1)}, bf16[256,1536]{1,0:T(8,128)(2,1)S(1)}, bf16[256,1536]{1,0:T(8,128)(2,1)S(1)}) fusion(f32[256,1536]{1,0:T(8,128)S(1)} %fusion.13, f32[256,1536]{1,0:T(8,128)S(1)} %copy-done.7, bf16[256,2304]{1,0:T(8,128)(2,1)S(1)} %bitcast.90, bf16[1,2304,1536]{2,1,0:T(8,128)(2,1)} %param.12), kind=kOutput, calls=%fused_computation.28 | convolution fusion | flops 1817837568 | bytes 13762560 | tf_op jit(solution)/shard_map/dot_general | solution.py:17
  75.6 2.0 fusion.15
  77.7 2.1 fusion.7
  79.8 2.0 fusion.18
  81.8 2.5 %pad_maximum_fusion = f32[2,4,64,2304]{3,2,1,0:T(8,128)} fusion(f32[1,4,64,2304]{3,2,1,0:T(8,128)S(1)} %bitcast.95, f32[1,4,64,2304]{3,2,1,0:T(8,128)S(1)} %fusion.15), kind=kLoop, calls=%fused_computation.19 | loop fusion | flops 1179648 | bytes 9437184 | tf_op jit(solution)/shard_map/stack | solution.py:120
  84.4 47.9 %reduce-scatter.2.cloned.1.call-done = f32[2,4,16,2304]{3,2,1,0:T(8,128)} async-done(((f32[2,4,64,2304]{3,2,1,0:T(8,128)}), f32[2,4,16,2304]{3,2,1,0:T(8,128)}) %reduce-scatter.2.cloned.1.call-update) | async-done | bytes 1179664 | tf_op jit(solution)/shard_map/reduce_scatter | solution.py:57
  132.3 1.3 copy.34
  133.7 33.0 %all_to_all.17 = f32[2,4,16,2304]{3,2,0,1:T(8,128)} all-to-all(f32[2,4,16,2304]{3,2,0,1:T(8,128)S(1)} %copy.34), channel_id=1, replica_groups=mesh['rep'=2,'grp'=4,'hid'=4] {'grp'}, dimensions={1} | all-to-all | bytes 2359296 | tf_op jit(solution)/shard_map/all_to_all | solution.py:58
  166.9 0.1 copy.33
  167.4 6.8 %fusion.2 = bf16[1,1536,2304]{2,1,0:T(8,128)(2,1)} fusion(bf16[256,1536]{1,0:T(8,128)(2,1)S(1)} %get-tuple-element.7, bf16[256,2304]{1,0:T(8,128)(2,1)} %bitcast.98), kind=kOutput, calls=%fused_computation.6 | convolution fusion | flops 1815478272 | bytes 9043968 | tf_op jit(solution)/shard_map/dot_general | solution.py:39
  174.2 5.0 %fusion = bf16[1,2304,1536]{2,1,0:T(8,128)(2,1)} fusion(bf16[256,2304]{1,0:T(8,128)(2,1)S(1)} %bitcast.91, bf16[256,1536]{1,0:T(8,128)(2,1)S(1)} %copy-done.4), kind=kOutput, calls=%fused_computation.4 | convolution fusion | flops 1815478272 | bytes 9043968 | tf_op jit(solution)/shard_map/dot_general | solution.py:33
  179.2 5.0 %fusion.1 = bf16[1,2304,1536]{2,1,0:T(8,128)(2,1)} fusion(bf16[256,2304]{1,0:T(8,128)(2,1)S(1)} %bitcast.92, bf16[256,1536]{1,0:T(8,128)(2,1)S(1)} %get-tuple-element.9), kind=kOutput, calls=%fused_computation.5 | convolution fusion | flops 1815478272 | bytes 9043968 | tf_op jit(solution)/shard_map/dot_general | solution.py:36
  184.2 18.4 %all-gather.8.cloned.1.call-done = f32[2,4,64,2304]{3,2,0,1:T(8,128)} async-done(((f32[2,4,16,2304]{3,2,0,1:T(8,128)}), f32[2,4,64,2304]{3,2,0,1:T(8,128)}) %all-gather.8.cloned.1.call-update) | async-done | bytes 4718608 | tf_op jit(solution)/shard_map/all_gather | solution.py:59
  202.5 8.2 %copy.35 = f32[2,4,64,2304]{3,0,2,1:T(2,128)} copy(f32[2,4,64,2304]{3,2,0,1:T(8,128)} %all-gather.8.cloned.1.call-done) | data formatting | bytes 9437184 | tf_op jit(solution)/shard_map/all_gather | solution.py:59
  210.7 4.2 %gather_fusion = f32[64,2,2304]{2,1,0:T(2,128)S(1)} fusion(f32[2,256,2304]{2,0,1:T(2,128)} %bitcast.93, s32[1024]{0:T(1024)S(1)} %pad_clamp_fusion), kind=kCustom, calls=%fused_computation | custom fusion | bytes 2359552 | tf_op jit(solution)/shard_map/jit(_take)/gather | solution.py:47
  214.9 1.1 multiply_reduce_fusion
  216.0 0.4 fusion.32
  216.4 0.7 copy_bitcast_fusion
  (60 shorter events, 1.5 us)
Async XLA Ops:
  7.2 21.6 %copy-start = (bf16[128,2304]{1,0:T(8,128)(2,1)S(1)}, bf16[128,2304]{1,0:T(8,128)(2,1)}, u32[]{:S(2)}) copy-start(bf16[128,2304]{1,0:T(8,128)(2,1)} %param.7) | copy-start | bytes 1769476
  7.2 5.1 %copy-start.6 = (f32[128,2]{0,1:T(2,128)S(1)}, f32[128,2]{0,1:T(2,128)}, u32[]{:S(2)}) copy-start(f32[128,2]{0,1:T(2,128)} %param.9) | copy-start | bytes 3076
  7.2 38.2 %all-gather.6.cloned.1.call-start = ((), (), s32[]{:S(2)}) async-start(), calls=%async_computation.5 | async-start | bytes 1474560 | tf_op jit(solution)/shard_map/all_gather | solution.py:104
  28.7 35.8 %all-gather.4.cloned.1.call-start = ((), (), s32[]{:S(2)}) async-start(), calls=%async_computation.4 | async-start | bytes 1474560 | tf_op jit(solution)/shard_map/all_gather | solution.py:103
  40.7 91.6 %reduce-scatter.2.cloned.1.call-start = ((), (), s32[]{:S(2)}) async-start(), calls=%async_computation.6 | async-start | bytes 5898240 | tf_op jit(solution)/shard_map/reduce_scatter | solution.py:57
  64.5 5.5 %copy-start.2 = (bf16[4,64,2304]{2,1,0:T(8,128)(2,1)S(1)}, bf16[4,64,2304]{2,1,0:T(8,128)(2,1)}, u32[]{:S(2)}) copy-start(bf16[4,64,2304]{2,1,0:T(8,128)(2,1)} %all-gather.4.cloned.1.call-done) | copy-start | bytes 3538948
  64.5 5.5 %copy-start.7 = (f32[256,1536]{1,0:T(8,128)S(1)}, f32[256,1536]{1,0:T(8,128)}, u32[]{:S(2)}) copy-start(f32[256,1536]{1,0:T(8,128)} %fusion.5) | copy-start | bytes 4718596
  64.5 11.1 %slice-start = ((s8[7077888]{0:T(1024)(128)(4,1)}), s8[4194304]{0:T(1024)(128)(4,1)S(1)}, s32[]{:S(2)}) async-start(s8[7077888]{0:T(1024)(128)(4,1)} %bitcast.106), calls=%async_computation.8 | async-start | bytes 8388608
  64.5 13.1 %slice-start.2 = ((s8[7077888]{0:T(1024)(128)(4,1)}), s8[4194304]{0:T(1024)(128)(4,1)S(1)}, s32[]{:S(2)}) async-start(s8[7077888]{0:T(1024)(128)(4,1)} %bitcast.108), calls=%async_computation.10 | async-start | bytes 8388608
  70.0 5.6 %slice-start.1 = ((s8[7077888]{0:T(1024)(128)(4,1)}), s8[2883584]{0:T(1024)(128)(4,1)S(1)}, s32[]{:S(2)}) async-start(s8[7077888]{0:T(1024)(128)(4,1)} %bitcast.106), calls=%async_computation.9 | async-start | bytes 5767168
  70.0 7.6 %slice-start.3 = ((s8[7077888]{0:T(1024)(128)(4,1)}), s8[2883584]{0:T(1024)(128)(4,1)S(1)}, s32[]{:S(2)}) async-start(s8[7077888]{0:T(1024)(128)(4,1)} %bitcast.108), calls=%async_computation.11 | async-start | bytes 5767168
  75.6 4.2 %copy-start.3 = (bf16[256,1536]{1,0:T(8,128)(2,1)}, bf16[256,1536]{1,0:T(8,128)(2,1)S(1)}, u32[]{:S(2)}) copy-start(bf16[256,1536]{1,0:T(8,128)(2,1)S(1)} %get-tuple-element.8) | copy-start | bytes 2359300
  75.6 4.1 %slice-start.4 = ((s8[7077888]{0:T(1024)(128)(4,1)}), s8[4194304]{0:T(1024)(128)(4,1)S(1)}, s32[]{:S(2)}) async-start(s8[7077888]{0:T(1024)(128)(4,1)} %bitcast.110), calls=%async_computation.12 | async-start | bytes 8388608
  77.6 2.1 slice-start.5
  84.4 118.2 %all-gather.8.cloned.1.call-start = ((), (), s32[]{:S(2)}) async-start(), calls=%async_computation.7 | async-start | bytes 5898240 | tf_op jit(solution)/shard_map/all_gather | solution.py:59
  133.7 33.1 %copy-start.5 = (s32[128,2]{0,1:T(2,128)S(1)}, s32[128,2]{0,1:T(2,128)}, u32[]{:S(2)}) copy-start(s32[128,2]{0,1:T(2,128)} %param.8) | copy-start | bytes 3076
  167.4 6.8 %copy-start.4 = (bf16[256,1536]{1,0:T(8,128)(2,1)S(1)}, bf16[256,1536]{1,0:T(8,128)(2,1)}, u32[]{:S(2)}) copy-start(bf16[256,1536]{1,0:T(8,128)(2,1)} %copy-done.3) | copy-start | bytes 2359300
  210.7 6.5 %copy-start.1 = (bf16[128,2304]{1,0:T(8,128)(2,1)S(1)}, bf16[128,2304]{1,0:T(8,128)(2,1)}, u32[]{:S(2)}) copy-start(bf16[128,2304]{1,0:T(8,128)(2,1)} %param.7) | copy-start | bytes 1769476
Sparse Core Ops, SparseCore 0:
  28.8 16.5 all-gather.5
  47.0 17.4 all-gather.3
  84.5 47.8 reduce-scatter.1
  166.9 35.5 all-gather.7
where the time goes:
time: 224 us
  waiting for transfers between devices  83.5 us (37%)
  blocking collectives  60.3 us (27%)
  matrix products  41.1 us (18%)
  local copies, waits for them, and re-layouts  16 us (7%)
  between operations  14.1 us (6%)
  other arithmetic  8.49 us (4%)
    reduce_scatter x1, waiting for transfers between devices, send_back(): summed = lax.psum_scatter(stacked, 'hid', scatter_dimension=2, tiled=True)  47.9 us
    all_to_all x1, blocking collectives, send_back(): lax.all_to_all(summed, 'grp', split_axis=1, concat_axis=1, tiled=True)  33 us
    all_gather x1, waiting for transfers between devices, send_back(): whole = lax.all_gather(moved, 'hid', axis=2, tiled=True)  18.4 us
    all_to_all x1, blocking collectives, local(): lax.all_to_all(send_c, 'grp', split_axis=0, concat_axis=0, tiled=True)  15.8 us
    all_gather x1, waiting for transfers between devices, local(): lax.all_gather(arrived[0], 'hid', axis=1, tiled=True)  12.5 us
    all_to_all x1, blocking collectives, local(): lax.all_to_all(send_x, 'grp', split_axis=0, concat_axis=0, tiled=True)  11.5 us
    all_gather x1, local copies, waits for them, and re-layouts, send_back(): whole = lax.all_gather(moved, 'hid', axis=2, tiled=True)  8.16 us
    dot_general x1, matrix products, backward_rows(): jnp.dot(hidden.T, rows_c, preferred_element_type=jnp.float32)  6.77 us
  transfers between devices with their start and end apart: 4, of which 4 were waited for; matrix products, arithmetic and copies ran while one was open for 11% of the time, Pallas kernels for 0%

commit v1 on v0

--- a/solution.py
+++ b/solution.py
@@ -1,7 +1,389 @@
+import functools
+
 import jax
 import jax.numpy as jnp
 from jax import lax
+from jax.experimental import pallas as pl
+from jax.experimental.pallas import tpu as pltpu
 from jax.sharding import PartitionSpec as P
+
+MESH = pl.DeviceIdType.MESH
+F32 = jnp.float32
+BF16 = jnp.bfloat16
+
+
+def nn(a, b):
+    return jnp.dot(a, b, preferred_element_type=F32)
+
+
+def nt(a, b):
+    return lax.dot_general(a, b, (((1,), (1,)), ((), ())), preferred_element_type=F32)
+
+
+def layer_kernel(
+    groups, quarter, tile,
+    tok, routes, gates, gout, wg_any, wu_any, wd_any,
+    x_any, c_any, hid_any, gpg_any, gpu_any, mixed_out, gtok_out,
+    wg, wu, wd, rows_x, rows_c, send, places, picks, silu, upslope, hidden, gpg, gpu,
+    acc, pair_send, pair_recv, x_send, x_recv, z_send, home, out_send, out_full,
+    zs, zr, xs, xr, cs, cr, c2s, c2r, x2s, x2r, z2s, z2r, h2s, h2r, os_, or_, wsem, lsem,
+):
+    rep = lax.axis_index("rep")
+    g = lax.axis_index("grp")
+    h = lax.axis_index("hid")
+    x = h // 2
+    c = lax.rem(h, 2)
+    over = (1 - x) * 2 + c
+    sib = x * 2 + 1 - c
+    tokens, width = tok.shape
+    hc = width // 2
+    gq = groups * quarter
+    ff = hidden.shape[1]
+    share = tokens // 4
+    xcols = pl.ds(pl.multiple_of(x * hc, 128), hc)
+    ocols = pl.ds(pl.multiple_of((1 - x) * hc, 128), hc)
+    rows = (rows_x, rows_c)
+
+    loads = [
+        pltpu.make_async_copy(a, b, wsem.at[i])
+        for i, (a, b) in enumerate(((wg_any, wg), (wu_any, wu), (wd_any, wd)))
+    ]
+    for load in loads:
+        load.start()
+
+    def group_of(shift):
+        return lax.rem(g + shift + groups, groups)
+
+    def block(half, group):
+        return pl.ds(pl.multiple_of(half * gq + group * quarter, 16), quarter)
+
+    def remote(src, dst, s_sem, r_sem, grp, hid):
+        return pltpu.make_async_remote_copy(
+            src_ref=src, dst_ref=dst, send_sem=s_sem, recv_sem=r_sem,
+            device_id=(rep, grp, hid), device_id_type=MESH,
+        )
+
+    barrier = pltpu.get_barrier_semaphore()
+    peers = [(group_of(i), h) for i in range(1, groups)] + [(g, over), (g, sib)]
+    for grp, hid in peers:
+        pl.semaphore_signal(barrier, inc=1, device_id=(rep, grp, hid), device_id_type=MESH)
+
+    pairs = 2 * tokens
+    named = jnp.concatenate([routes[:, 0:1], routes[:, 1:2]], axis=0)
+    onehot = named == lax.broadcasted_iota(jnp.int32, (pairs, 128), 1)
+    before = lax.broadcasted_iota(jnp.int32, (pairs, pairs), 0) > lax.broadcasted_iota(
+        jnp.int32, (pairs, pairs), 1
+    )
+    earlier = nn(before.astype(F32).astype(BF16), onehot.astype(F32).astype(BF16))
+    slot = jnp.sum(jnp.where(onehot, earlier, 0.0), axis=1, keepdims=True).astype(jnp.int32)
+    upper = (slot >= quarter).astype(jnp.int32)
+    place = upper * (gq - quarter) + named * quarter + slot
+    at = (place == lax.broadcasted_iota(jnp.int32, (pairs, 2 * gq), 1)).astype(F32)
+    picks[...] = at.astype(BF16)
+    places[...] = at.T.astype(BF16)
+
+    pl.semaphore_wait(barrier, len(peers))
+
+    def cot(cols):
+        wide = gout[:, cols].astype(F32)
+        return jnp.concatenate(
+            [(gates[:, 0:1] * wide).astype(BF16), (gates[:, 1:2] * wide).astype(BF16)], axis=0
+        )
+
+    def z_copy(k, i):
+        dest = group_of(i)
+        return remote(
+            send.at[k, pl.ds(pl.multiple_of(dest * quarter, 16), quarter), :],
+            rows[k].at[block(c, g), xcols], zs.at[k, i], zr.at[k, i], dest, h,
+        )
+
+    def x_copy(k, i):
+        ref = rows[k].at[block(c, group_of(-i)), xcols]
+        return remote(ref, ref, xs.at[k, i], xr.at[k, i], g, over)
+
+    def c_copy(k, i):
+        ref = rows[k].at[block(c, group_of(-i)), :]
+        return remote(ref, ref, cs.at[k, i], cr.at[k, i], g, sib)
+
+    others = range(1, groups)
+    mine = places[pl.ds(pl.multiple_of(c * gq, 16), gq), :]
+    send[0] = nn(mine[:, :tokens] + mine[:, tokens:], tok[:, xcols]).astype(BF16)
+    for i in others:
+        z_copy(0, i).start()
+    send[1] = nn(mine, cot(xcols)).astype(BF16)
+    for i in others:
+        z_copy(1, i).start()
+    for half in range(2):
+        own = places[block(half, g), :]
+        rows_x[block(half, g), :] = nn(own[:, :tokens] + own[:, tokens:], tok[...]).astype(BF16)
+        for n in range(2):
+            cols = slice(n * hc, n * hc + hc)
+            rows_c[block(half, g), cols] = nn(own, cot(cols)).astype(BF16)
+
+    def pass_over(k):
+        for i in others:
+            z_copy(k, i).wait_recv()
+            x_copy(k, i).start()
+
+    def pass_sib(k):
+        for i in others:
+            x_copy(k, i).wait_recv()
+            c_copy(k, i).start()
+
+    def arrived(k):
+        for i in others:
+            c_copy(k, i).wait_recv()
+
+    pass_over(0)
+    pass_sib(0)
+    arrived(0)
+    pass_over(1)
+
+    def at_tile(n):
+        return pl.ds(pl.multiple_of(n * tile, tile), tile)
+
+    stores = []
+
+    def store(src, dst):
+        stores.append(pltpu.make_async_copy(src, dst, lsem.at[len(stores)]))
+        stores[-1].start()
+
+    store(rows_x, x_any)
+    loads[0].wait()
+    loads[1].wait()
+
+    @pl.loop(0, ff // tile)
+    def _(n):
+        cols = at_tile(n)
+        gate = nn(rows_x[...], wg[:, cols])
+        up = nn(rows_x[...], wu[:, cols])
+        sigma = jax.nn.sigmoid(gate)
+        act = gate * sigma
+        silu[:, cols] = act
+        upslope[:, cols] = up * (sigma * (1.0 + gate * (1.0 - sigma)))
+        hidden[:, cols] = (act * up).astype(BF16)
+
+    store(hidden, hid_any)
+    pass_sib(1)
+    loads[2].wait()
+    other_rows = pl.ds(pl.multiple_of((1 - c) * gq, 16), gq)
+
+    @pl.loop(0, width // tile)
+    def _(n):
+        cols = at_tile(n)
+        acc[0, :, cols] = nn(hidden[...], wd[:, cols])
+        pair_send[0, :, cols] = acc[0, other_rows, cols].astype(BF16)
+
+    def part(group):
+        return pl.ds(pl.multiple_of(group * quarter, 16), quarter)
+
+    def pair_copy(k, i):
+        at_ = part(group_of(i))
+        return remote(
+            pair_send.at[k, at_, :], pair_recv.at[k, at_, :], c2s.at[k, i], c2r.at[k, i], g, sib
+        )
+
+    def cross_copy(k, i):
+        at_ = part(group_of(i))
+        return remote(
+            x_send.at[k, at_, :], x_recv.at[k, at_, :], x2s.at[k, i], x2r.at[k, i], g, over
+        )
+
+    def home_copy(k, i):
+        dest = group_of(i)
+        return remote(
+            z_send.at[k, part(dest), :], home.at[k, block(c, g), :],
+            z2s.at[k, i], z2r.at[k, i], dest, h,
+        )
+
+    def twin_copy(k, i):
+        ref = home.at[k, block(c, group_of(-i)), :]
+        return remote(ref, ref, h2s.at[k, i], h2r.at[k, i], g, sib)
+
+    order = list(others) + [0]
+
+    def start_pair(k):
+        for i in order:
+            pair_copy(k, i).start()
+
+    def cross(k):
+        for i in order:
+            pair_copy(k, i).wait_recv()
+            here, there = block(c, group_of(i)), part(group_of(i))
+            x_send[k, there, :] = (
+                acc[k, here, ocols] + pair_recv[k, there, ocols].astype(F32)
+            ).astype(BF16)
+            cross_copy(k, i).start()
+            acc[k, here, xcols] = acc[k, here, xcols] + pair_recv[k, there, xcols].astype(F32)
+
+    def go_home(k):
+        for i in order:
+            cross_copy(k, i).wait_recv()
+            here, there = block(c, group_of(i)), part(group_of(i))
+            total = (acc[k, here, xcols] + x_recv[k, there, :].astype(F32)).astype(BF16)
+            if i == 0:
+                home[k, here, :] = total
+                twin_copy(k, 0).start()
+            else:
+                z_send[k, there, :] = total
+                home_copy(k, i).start()
+
+    def twin(k):
+        for i in others:
+            home_copy(k, i).wait_recv()
+            twin_copy(k, i).start()
+
+    def out_copy(k):
+        return remote(
+            out_send.at[k], out_full.at[k, :, xcols], os_.at[k], or_.at[k], g, over
+        )
+
+    def combine(k):
+        for i in order:
+            twin_copy(k, i).wait_recv()
+        for to in (1 - x, x):
+            base = pl.multiple_of(to * (2 * share) + c * share, 16)
+            first = picks[pl.ds(base, share), :]
+            second = picks[pl.ds(base + tokens, share), :]
+            if k == 0:
+                w = gates[pl.ds(base, share), :]
+                value = w[:, 0:1] * nn(first, home[0]) + w[:, 1:2] * nn(second, home[0])
+            else:
+                value = nn(first + second, home[1])
+            if to is x:
+                out_full[k, :, xcols] = value.astype(BF16)
+            else:
+                out_send[k] = value.astype(BF16)
+                out_copy(k).start()
+
+    start_pair(0)
+    arrived(1)
+    store(rows_c, c_any)
+
+    @pl.loop(0, ff // tile)
+    def _(n):
+        cols = at_tile(n)
+        back = nt(rows_c[...], wd[cols, :])
+        gpg[:, cols] = (back * upslope[:, cols]).astype(BF16)
+        gpu[:, cols] = (back * silu[:, cols]).astype(BF16)
+
+    store(gpg, gpg_any)
+    store(gpu, gpu_any)
+    cross(0)
+
+    @pl.loop(0, width // tile)
+    def _(n):
+        cols = at_tile(n)
+        acc[1, :, cols] = nt(gpg[...], wg[cols, :]) + nt(gpu[...], wu[cols, :])
+        pair_send[1, :, cols] = acc[1, other_rows, cols].astype(BF16)
+
+    start_pair(1)
+    go_home(0)
+    cross(1)
+    go_home(1)
+    twin(0)
+    combine(0)
+    twin(1)
+    combine(1)
+    for k in range(2):
+        out_copy(k).wait_recv()
+    mixed_out[...] = out_full[0]
+    gtok_out[...] = out_full[1]
+
+    for k in range(2):
+        for i in others:
+            z_copy(k, i).wait_send()
+            x_copy(k, i).wait_send()
+            c_copy(k, i).wait_send()
+            home_copy(k, i).wait_send()
+        for i in order:
+            pair_copy(k, i).wait_send()
+            cross_copy(k, i).wait_send()
+            twin_copy(k, i).wait_send()
+        out_copy(k).wait_send()
+    for s in stores:
+        s.wait()
+
+
+def fits(tokens, capacity, shares, width, ff):
+    return (
+        shares == 4
+        and capacity % 32 == 0
+        and tokens % 64 == 0
+        and width % 256 == 0
+        and ff % 256 == 0
+    )
+
+
+def local_fused(tokens, routes, gates, grad_out, w_gate, w_up, w_down):
+    groups = lax.axis_size("grp")
+    tok_rows, width = tokens.shape
+    ff = w_gate.shape[2]
+    capacity = capacity_of(tok_rows, routes.shape[1], groups)
+    quarter = capacity // 2
+    tile = 256
+    rows = groups * capacity
+    half_rows, hc = rows // 2, width // 2
+    share = tok_rows // 4
+    vmem = pl.BlockSpec(memory_space=pltpu.VMEM)
+    hbm = pl.BlockSpec(memory_space=pl.ANY)
+    dma = pltpu.SemaphoreType.DMA
+    flops = 2 * rows * width * ff * 6
+    rows_x, rows_c, hidden, gpg, gpu, mixed, grad_tokens = pl.pallas_call(
+        functools.partial(layer_kernel, groups, quarter, tile),
+        out_shape=[
+            jax.ShapeDtypeStruct((rows, width), BF16),
+            jax.ShapeDtypeStruct((rows, width), BF16),
+            jax.ShapeDtypeStruct((rows, ff), BF16),
+            jax.ShapeDtypeStruct((rows, ff), BF16),
+            jax.ShapeDtypeStruct((rows, ff), BF16),
+            jax.ShapeDtypeStruct((share, width), BF16),
+            jax.ShapeDtypeStruct((share, width), BF16),
+        ],
+        in_specs=[vmem] * 4 + [hbm] * 3,
+        out_specs=[hbm] * 5 + [vmem] * 2,
+        scratch_shapes=[
+            pltpu.VMEM((width, ff), BF16),
+            pltpu.VMEM((width, ff), BF16),
+            pltpu.VMEM((ff, width), BF16),
+            pltpu.VMEM((rows, width), BF16),
+            pltpu.VMEM((rows, width), BF16),
+            pltpu.VMEM((2, half_rows, hc), BF16),
+            pltpu.VMEM((rows, 2 * tok_rows), BF16),
+            pltpu.VMEM((2 * tok_rows, rows), BF16),
+            pltpu.VMEM((rows, ff), F32),
+            pltpu.VMEM((rows, ff), F32),
+            pltpu.VMEM((rows, ff), BF16),
+            pltpu.VMEM((rows, ff), BF16),
+            pltpu.VMEM((rows, ff), BF16),
+            pltpu.VMEM((2, rows, width), F32),
+            pltpu.VMEM((2, half_rows, width), BF16),
+            pltpu.VMEM((2, half_rows, width), BF16),
+            pltpu.VMEM((2, half_rows, hc), BF16),
+            pltpu.VMEM((2, half_rows, hc), BF16),
+            pltpu.VMEM((2, half_rows, hc), BF16),
+            pltpu.VMEM((2, rows, hc), BF16),
+            pltpu.VMEM((2, share, hc), BF16),
+            pltpu.VMEM((2, share, width), BF16),
+        ]
+        + [dma((2, groups))] * 14
+        + [dma((2,)), dma((2,)), dma((3,)), dma((5,))],
+        compiler_params=pltpu.CompilerParams(
+            collective_id=0, has_side_effects=True, vmem_limit_bytes=56 * 1024 * 1024
+        ),
+        cost_estimate=pl.CostEstimate(
+            flops=flops, bytes_accessed=6 * width * ff, transcendentals=rows * ff
+        ),
+    )(tokens, routes, gates, grad_out, w_gate[0], w_up[0], w_down[0])
+    grads = [
+        lax.dot_general(a, b, (((0,), (0,)), ((), ())), preferred_element_type=F32).astype(BF16)
+        for a, b in ((rows_x, gpg), (rows_x, gpu), (hidden, rows_c))
+    ]
+    return (mixed, grad_tokens, grads[0][None], grads[1][None], grads[2][None])
+
+
+def capacity_of(tok_rows, top_count, groups):
+    return max(3 * tok_rows // 8, top_count * tok_rows // groups)
 
 
 def slot_numbers(route_blocks, expert_count):
@@ -63,7 +445,7 @@
     return combine_pairs(whole, own_weights, own_rows)
 
 
-def local(tokens, routes, gates, grad_out, w_gate, w_up, w_down):
+def local_plain(tokens, routes, gates, grad_out, w_gate, w_up, w_down):
     groups = lax.axis_size("grp")
     shares = lax.axis_size("hid")
     share = lax.axis_index("hid")
@@ -126,6 +508,15 @@
     return (mixed, grad_tokens, grad_wgate[None], grad_wup[None], grad_wdown[None])
 
 
+def local(tokens, routes, gates, grad_out, w_gate, w_up, w_down):
+    capacity = capacity_of(tokens.shape[0], routes.shape[1], lax.axis_size("grp"))
+    args = (tokens, routes, gates, grad_out, w_gate, w_up, w_down)
+    shares = lax.axis_size("hid")
+    if fits(tokens.shape[0], capacity, shares, tokens.shape[1], w_gate.shape[2]):
+        return local_fused(*args)
+    return local_plain(*args)
+
+
 def solution(mesh):
     in_specs = (
         P(("rep", "grp"), None),

time: 224 us -> 81.7 us (0.36)
  waiting for transfers between devices: 83.5 us -> 0 us
  blocking collectives: 60.3 us -> 0 us
  Pallas kernels: 0 us -> 60 us
  matrix products: 41.1 us -> 16.7 us
  between operations: 14.1 us -> 0.68 us
  local copies, waits for them, and re-layouts: 16 us -> 4.17 us
  other arithmetic: 8.49 us -> 0 us
    all_to_all x3 -> x0, blocking collectives: 60.3 us -> none  [the longest x1 33 us: send_back(): lax.all_to_all(summed, 'grp', split_axis=1, concat_axis=1, tiled=True)]
    pallas_call x0 -> x1, Pallas kernels: none -> 60 us  [local_fused(): pl.pallas_call(functools.partial(layer_kernel, groups, quarter, tile), ou...]
    reduce_scatter x1 -> x0, waiting for transfers between devices: 47.9 us -> none  [send_back(): summed = lax.psum_scatter(stacked, 'hid', scatter_dimension=2, tiled=True)]
    all_gather x3 -> x0, waiting for transfers between devices: 35.5 us -> none  [the longest x1 18.4 us: send_back(): whole = lax.all_gather(moved, 'hid', axis=2, tiled=True)]
    dot_general x11 -> x3, matrix products: 41.1 us -> 16.7 us  [local_fused(): lax.dot_general(a, b, (((0,), (0,)), ((), ())), preferred_element_type=F32)]
    all_gather x1 -> x0, local copies, waits for them, and re-layouts: 8.16 us -> none  [send_back(): whole = lax.all_gather(moved, 'hid', axis=2, tiled=True)]
    gather x1 -> x0, local copies, waits for them, and re-layouts: 4.23 us -> none  [combine_pairs(): jnp.take(flat, row_ids.reshape(-1), axis=1)]
    another operation x3 -> x0, other arithmetic: 3.79 us -> none  [the longest x1 2.55 us: local(): jnp.stack([out_terms, grad_rows.reshape(block_shape)])]
  transfers between devices with their start and end apart: 4 -> 0, of which waited for: 4 -> 0; matrix products, arithmetic and copies ran while one was open for 11% -> 0% of each run, Pallas kernels for 0% -> 0%
where the time goes in v1:
time: 81.7 us; the launch traced here: 81.6 us
  Pallas kernels  60 us (73%)
  matrix products  16.7 us (20%)
  local copies, waits for them, and re-layouts  4.17 us (5%)
    pallas_call x1, Pallas kernels, local_fused(): pl.pallas_call(functools.partial(layer_kernel, groups, quarter, tile), ou...  60 us
    dot_general x3, matrix products, local_fused(): lax.dot_general(a, b, (((0,), (0,)), ((), ())), preferred_element_type=F32)  16.7 us
    unnamed x16, local copies, waits for them, and re-layouts  4.17 us

profile of v1, /device:TPU:0, one launch (start us, length us, event | category | flops | bytes accessed | tf_op | source)
XLA Modules:
  0.0 81.6 jit_solution(6161640244312722087)
XLA Ops:
  0.6 1.4 %copy.12.routes = s32[128,2]{1,0:T(8,128)} copy(s32[128,2]{0,1:T(2,128)} %param.8) | data formatting | bytes 2048 | tf_op args[1]
  2.0 1.4 %copy.13.gates = f32[128,2]{1,0:T(8,128)} copy(f32[128,2]{0,1:T(2,128)} %param.9) | data formatting | bytes 2048 | tf_op args[2]
  3.5 60.0 %shard_map.110 = (bf16[256,2304]{1,0:T(8,128)(2,1)}, bf16[256,2304]{1,0:T(8,128)(2,1)}, bf16[256,1536]{1,0:T(8,128)(2,1)}, bf16[256,1536]{1,0:T(8,128)(2,1)}, bf...) custom-call(bf16[128,2304]{1,0:T(8,128)(2,1)} %tok.1, s32[128,2]{1,0:T(8,128)} %copy.12.routes, ...), custom_call_target="tpu_custom_call" | custom-call | flops 10871635968 | bytes 21233664 | tf_op jit(solution)/shard_map/pallas_call | solution.py:332
  63.5 0.0 copy-start
  63.5 0.0 copy-start.3
  63.5 0.0 copy-start.1
  63.5 0.0 copy-start.2
  63.5 6.6 %fusion = bf16[1,2304,1536]{2,1,0:T(8,128)(2,1)} fusion(bf16[256,2304]{1,0:T(8,128)(2,1)} %get-tuple-element.14, bf16[256,1536]{1,0:T(8,128)(2,1)} %get-tuple-element.15), kind=kOutput, calls=%fused_computation.3 | convolution fusion | flops 1815478272 | bytes 9043968 | tf_op jit(solution)/shard_map/dot_general | solution.py:379
  70.2 0.0 copy-done
  70.2 0.0 copy-done.3
  70.2 0.0 copy-start.5
  70.2 5.0 %fusion.1 = bf16[1,2304,1536]{2,1,0:T(8,128)(2,1)} fusion(bf16[256,2304]{1,0:T(8,128)(2,1)S(1)} %copy-done, bf16[256,1536]{1,0:T(8,128)(2,1)S(1)} %copy-done.3), kind=kOutput, calls=%fused_computation.4 | convolution fusion | flops 1815478272 | bytes 9043968 | tf_op jit(solution)/shard_map/dot_general | solution.py:379
  75.2 0.0 copy-done.1
  75.2 0.0 copy-done.2
  75.2 0.0 copy-start.4
  75.2 5.0 %fusion.2 = bf16[1,1536,2304]{2,1,0:T(8,128)(2,1)} fusion(bf16[256,1536]{1,0:T(8,128)(2,1)S(1)} %copy-done.1, bf16[256,2304]{1,0:T(8,128)(2,1)S(1)} %copy-done.2), kind=kOutput, calls=%fused_computation.5 | convolution fusion | flops 1815478272 | bytes 9043968 | tf_op jit(solution)/shard_map/dot_general | solution.py:379
  80.2 0.0 copy-done.5
  80.2 0.7 copy.16
  80.9 0.0 copy-done.4
  80.9 0.7 copy.17
Async XLA Ops:
  63.5 6.7 %copy-start = (bf16[256,2304]{1,0:T(8,128)(2,1)S(1)}, bf16[256,2304]{1,0:T(8,128)(2,1)}, u32[]{:S(2)}) copy-start(bf16[256,2304]{1,0:T(8,128)(2,1)} %get-tuple-element.14) | copy-start | bytes 3538948
  63.5 6.7 %copy-start.3 = (bf16[256,1536]{1,0:T(8,128)(2,1)S(1)}, bf16[256,1536]{1,0:T(8,128)(2,1)}, u32[]{:S(2)}) copy-start(bf16[256,1536]{1,0:T(8,128)(2,1)} %get-tuple-element.16) | copy-start | bytes 2359300
  63.5 11.7 %copy-start.1 = (bf16[256,1536]{1,0:T(8,128)(2,1)S(1)}, bf16[256,1536]{1,0:T(8,128)(2,1)}, u32[]{:S(2)}) copy-start(bf16[256,1536]{1,0:T(8,128)(2,1)} %get-tuple-element.17) | copy-start | bytes 2359300
  63.5 11.7 %copy-start.2 = (bf16[256,2304]{1,0:T(8,128)(2,1)S(1)}, bf16[256,2304]{1,0:T(8,128)(2,1)}, u32[]{:S(2)}) copy-start(bf16[256,2304]{1,0:T(8,128)(2,1)} %get-tuple-element.18) | copy-start | bytes 3538948
  70.2 10.0 %copy-start.5 = (bf16[32,2304]{1,0:T(8,128)(2,1)S(1)}, bf16[32,2304]{1,0:T(8,128)(2,1)}, u32[]{:S(2)}) copy-start(bf16[32,2304]{1,0:T(8,128)(2,1)} %get-tuple-element.24) | copy-start | bytes 442372
  75.2 5.7 %copy-start.4 = (bf16[32,2304]{1,0:T(8,128)(2,1)S(1)}, bf16[32,2304]{1,0:T(8,128)(2,1)}, u32[]{:S(2)}) copy-start(bf16[32,2304]{1,0:T(8,128)(2,1)} %get-tuple-element.25) | copy-start | bytes 442372

commit v2 on v1

--- a/solution.py
+++ b/solution.py
@@ -12,6 +12,9 @@
 BF16 = jnp.bfloat16
 
 
+UNROLL = 8
+
+
 def nn(a, b):
     return jnp.dot(a, b, preferred_element_type=F32)
 
@@ -20,12 +23,21 @@
     return lax.dot_general(a, b, (((1,), (1,)), ((), ())), preferred_element_type=F32)
 
 
+def column(row):
+    size = row.shape[1]
+    square = (size, size)
+    diagonal = lax.broadcasted_iota(jnp.int32, square, 0) == lax.broadcasted_iota(
+        jnp.int32, square, 1
+    )
+    return jnp.sum(jnp.where(diagonal, row, 0.0), axis=1, keepdims=True)
+
+
 def layer_kernel(
     groups, quarter, tile,
-    tok, routes, gates, gout, wg_any, wu_any, wd_any,
-    x_any, c_any, hid_any, gpg_any, gpu_any, mixed_out, gtok_out,
+    tok, routes, gates_row, gout, wg_any, wu_any, wd_any,
+    xt_any, c_any, hidt_any, gpg_any, gpu_any, mixed_out, gtok_out,
     wg, wu, wd, rows_x, rows_c, send, places, picks, silu, upslope, hidden, gpg, gpu,
-    acc, pair_send, pair_recv, x_send, x_recv, z_send, home, out_send, out_full,
+    rows_xt, hidden_t, gates, acc, pair_send, pair_recv, x_send, x_recv, z_send, home, out_send, out_full,
     zs, zr, xs, xr, cs, cr, c2s, c2r, x2s, x2r, z2s, z2r, h2s, h2r, os_, or_, wsem, lsem,
 ):
     rep = lax.axis_index("rep")
@@ -69,7 +81,12 @@
         pl.semaphore_signal(barrier, inc=1, device_id=(rep, grp, hid), device_id_type=MESH)
 
     pairs = 2 * tokens
-    named = jnp.concatenate([routes[:, 0:1], routes[:, 1:2]], axis=0)
+    wide_routes = routes[...].astype(F32)
+    named = jnp.concatenate(
+        [column(wide_routes[0:1, :]), column(wide_routes[1:2, :])], axis=0
+    ).astype(jnp.int32)
+    for n in range(2):
+        gates[:, n : n + 1] = column(gates_row[n : n + 1, :])
     onehot = named == lax.broadcasted_iota(jnp.int32, (pairs, 128), 1)
     before = lax.broadcasted_iota(jnp.int32, (pairs, pairs), 0) > lax.broadcasted_iota(
         jnp.int32, (pairs, pairs), 1
@@ -111,8 +128,6 @@
     for i in others:
         z_copy(0, i).start()
     send[1] = nn(mine, cot(xcols)).astype(BF16)
-    for i in others:
-        z_copy(1, i).start()
     for half in range(2):
         own = places[block(half, g), :]
         rows_x[block(half, g), :] = nn(own[:, :tokens] + own[:, tokens:], tok[...]).astype(BF16)
@@ -135,6 +150,8 @@
             c_copy(k, i).wait_recv()
 
     pass_over(0)
+    for i in others:
+        z_copy(1, i).start()
     pass_sib(0)
     arrived(0)
     pass_over(1)
@@ -148,11 +165,10 @@
         stores.append(pltpu.make_async_copy(src, dst, lsem.at[len(stores)]))
         stores[-1].start()
 
-    store(rows_x, x_any)
     loads[0].wait()
     loads[1].wait()
 
-    @pl.loop(0, ff // tile)
+    @pl.loop(0, ff // tile, unroll=UNROLL)
     def _(n):
         cols = at_tile(n)
         gate = nn(rows_x[...], wg[:, cols])
@@ -163,12 +179,11 @@
         upslope[:, cols] = up * (sigma * (1.0 + gate * (1.0 - sigma)))
         hidden[:, cols] = (act * up).astype(BF16)
 
-    store(hidden, hid_any)
     pass_sib(1)
     loads[2].wait()
     other_rows = pl.ds(pl.multiple_of((1 - c) * gq, 16), gq)
 
-    @pl.loop(0, width // tile)
+    @pl.loop(0, width // tile, unroll=UNROLL)
     def _(n):
         cols = at_tile(n)
         acc[0, :, cols] = nn(hidden[...], wd[:, cols])
@@ -177,10 +192,12 @@
     def part(group):
         return pl.ds(pl.multiple_of(group * quarter, 16), quarter)
 
-    def pair_copy(k, i):
-        at_ = part(group_of(i))
+    def pair_copy(k, i, n):
+        at_, cols = part(group_of(i)), (ocols, xcols)[n]
+        j = i + n * groups
         return remote(
-            pair_send.at[k, at_, :], pair_recv.at[k, at_, :], c2s.at[k, i], c2r.at[k, i], g, sib
+            pair_send.at[k, at_, cols], pair_recv.at[k, at_, cols],
+            c2s.at[k, j], c2r.at[k, j], g, sib,
         )
 
     def cross_copy(k, i):
@@ -202,25 +219,28 @@
 
     order = list(others) + [0]
 
-    def start_pair(k):
+    def start_pair(k, n):
         for i in order:
-            pair_copy(k, i).start()
+            pair_copy(k, i, n).start()
 
     def cross(k):
         for i in order:
-            pair_copy(k, i).wait_recv()
+            pair_copy(k, i, 0).wait_recv()
             here, there = block(c, group_of(i)), part(group_of(i))
             x_send[k, there, :] = (
                 acc[k, here, ocols] + pair_recv[k, there, ocols].astype(F32)
             ).astype(BF16)
             cross_copy(k, i).start()
-            acc[k, here, xcols] = acc[k, here, xcols] + pair_recv[k, there, xcols].astype(F32)
 
     def go_home(k):
         for i in order:
+            pair_copy(k, i, 1).wait_recv()
             cross_copy(k, i).wait_recv()
             here, there = block(c, group_of(i)), part(group_of(i))
-            total = (acc[k, here, xcols] + x_recv[k, there, :].astype(F32)).astype(BF16)
+            total = (
+                (acc[k, here, xcols] + pair_recv[k, there, xcols].astype(F32))
+                + x_recv[k, there, :].astype(F32)
+            ).astype(BF16)
             if i == 0:
                 home[k, here, :] = total
                 twin_copy(k, 0).start()
@@ -256,31 +276,56 @@
                 out_send[k] = value.astype(BF16)
                 out_copy(k).start()
 
-    start_pair(0)
+    start_pair(0, 0)
+    start_pair(0, 1)
     arrived(1)
     store(rows_c, c_any)
 
-    @pl.loop(0, ff // tile)
-    def _(n):
-        cols = at_tile(n)
-        back = nt(rows_c[...], wd[cols, :])
-        gpg[:, cols] = (back * upslope[:, cols]).astype(BF16)
-        gpu[:, cols] = (back * silu[:, cols]).astype(BF16)
-
+    def back_tiles(first, last):
+        @pl.loop(first, last, unroll=UNROLL)
+        def _(n):
+            cols = at_tile(n)
+            back = nt(rows_c[...], wd[cols, :])
+            gpg[:, cols] = (back * upslope[:, cols]).astype(BF16)
+            gpu[:, cols] = (back * silu[:, cols]).astype(BF16)
+
+    tiles = ff // tile
+    back_tiles(0, tiles // 2)
+    cross(0)
+    back_tiles(tiles // 2, tiles)
     store(gpg, gpg_any)
     store(gpu, gpu_any)
-    cross(0)
+
+    def grad_cols(cols):
+        acc[1, :, cols] = nt(gpg[...], wg[cols, :]) + nt(gpu[...], wu[cols, :])
+        pair_send[1, :, cols] = acc[1, other_rows, cols].astype(BF16)
+
+    for n, side in enumerate((1 - x, x)):
+
+        @pl.loop(0, hc // tile, unroll=UNROLL)
+        def _(j):
+            grad_cols(pl.ds(pl.multiple_of(side * hc + j * tile, 128), tile))
+
+        rest = hc % tile
+        if rest:
+            grad_cols(pl.ds(pl.multiple_of(side * hc + hc - rest, 128), rest))
+        start_pair(1, n)
+
+    cross(1)
+    go_home(0)
 
     @pl.loop(0, width // tile)
     def _(n):
-        cols = at_tile(n)
-        acc[1, :, cols] = nt(gpg[...], wg[cols, :]) + nt(gpu[...], wu[cols, :])
-        pair_send[1, :, cols] = acc[1, other_rows, cols].astype(BF16)
-
-    start_pair(1)
-    go_home(0)
-    cross(1)
+        rows_xt[at_tile(n), :] = rows_x[:, at_tile(n)].T
+
+    store(rows_xt, xt_any)
     go_home(1)
+
+    @pl.loop(0, tiles)
+    def _(n):
+        hidden_t[at_tile(n), :] = hidden[:, at_tile(n)].T
+
+    store(hidden_t, hidt_any)
     twin(0)
     combine(0)
     twin(1)
@@ -297,12 +342,27 @@
             c_copy(k, i).wait_send()
             home_copy(k, i).wait_send()
         for i in order:
-            pair_copy(k, i).wait_send()
+            pair_copy(k, i, 0).wait_send()
+            pair_copy(k, i, 1).wait_send()
             cross_copy(k, i).wait_send()
             twin_copy(k, i).wait_send()
         out_copy(k).wait_send()
     for s in stores:
         s.wait()
+
+
+def weights_kernel(
+    rows_xt, hidden_t, gpg, gpu, rows_c, mixed, gtok,
+    mixed_out, gtok_out, grad_gate, grad_up, grad_down,
+):
+    @pl.when(pl.program_id(0) == 0)
+    def _():
+        mixed_out[...] = mixed[...]
+        gtok_out[...] = gtok[...]
+
+    grad_gate[...] = nn(rows_xt[...], gpg[...]).astype(BF16)
+    grad_up[...] = nn(rows_xt[...], gpu[...]).astype(BF16)
+    grad_down[...] = nn(hidden_t[...], rows_c[...]).astype(BF16)
 
 
 def fits(tokens, capacity, shares, width, ff):
@@ -329,12 +389,12 @@
     hbm = pl.BlockSpec(memory_space=pl.ANY)
     dma = pltpu.SemaphoreType.DMA
     flops = 2 * rows * width * ff * 6
-    rows_x, rows_c, hidden, gpg, gpu, mixed, grad_tokens = pl.pallas_call(
+    rows_xt, rows_c, hidden_t, gpg, gpu, mixed, grad_tokens = pl.pallas_call(
         functools.partial(layer_kernel, groups, quarter, tile),
         out_shape=[
+            jax.ShapeDtypeStruct((width, rows), BF16),
             jax.ShapeDtypeStruct((rows, width), BF16),
-            jax.ShapeDtypeStruct((rows, width), BF16),
-            jax.ShapeDtypeStruct((rows, ff), BF16),
+            jax.ShapeDtypeStruct((ff, rows), BF16),
             jax.ShapeDtypeStruct((rows, ff), BF16),
             jax.ShapeDtypeStruct((rows, ff), BF16),
             jax.ShapeDtypeStruct((share, width), BF16),
@@ -356,6 +416,9 @@
             pltpu.VMEM((rows, ff), BF16),
             pltpu.VMEM((rows, ff), BF16),
             pltpu.VMEM((rows, ff), BF16),
+            pltpu.VMEM((width, rows), BF16),
+            pltpu.VMEM((ff, rows), BF16),
+            pltpu.VMEM((tok_rows, 2), F32),
             pltpu.VMEM((2, rows, width), F32),
             pltpu.VMEM((2, half_rows, width), BF16),
             pltpu.VMEM((2, half_rows, width), BF16),
@@ -366,7 +429,9 @@
             pltpu.VMEM((2, share, hc), BF16),
             pltpu.VMEM((2, share, width), BF16),
         ]
-        + [dma((2, groups))] * 14
+        + [dma((2, groups))] * 6
+        + [dma((2, 2 * groups))] * 2
+        + [dma((2, groups))] * 6
         + [dma((2,)), dma((2,)), dma((3,)), dma((5,))],
         compiler_params=pltpu.CompilerParams(
             collective_id=0, has_side_effects=True, vmem_limit_bytes=56 * 1024 * 1024
@@ -374,12 +439,43 @@
         cost_estimate=pl.CostEstimate(
             flops=flops, bytes_accessed=6 * width * ff, transcendentals=rows * ff
         ),
-    )(tokens, routes, gates, grad_out, w_gate[0], w_up[0], w_down[0])
-    grads = [
-        lax.dot_general(a, b, (((0,), (0,)), ((), ())), preferred_element_type=F32).astype(BF16)
-        for a, b in ((rows_x, gpg), (rows_x, gpu), (hidden, rows_c))
-    ]
-    return (mixed, grad_tokens, grads[0][None], grads[1][None], grads[2][None])
+    )(tokens, routes.T, gates.T, grad_out, w_gate[0], w_up[0], w_down[0])
+    steps = 6 if ff % 768 == 0 and width % 768 == 0 else 2
+    wide, narrow = width // steps, ff // steps
+    whole = lambda shape: pl.BlockSpec(shape, lambda n: (0, 0))
+    side = lambda shape: pl.BlockSpec(shape, lambda n: (0, n))
+    mixed, grad_tokens, grad_gate, grad_up, grad_down = pl.pallas_call(
+        weights_kernel,
+        grid=(steps,),
+        out_shape=[
+            jax.ShapeDtypeStruct((share, width), BF16),
+            jax.ShapeDtypeStruct((share, width), BF16),
+            jax.ShapeDtypeStruct((width, ff), BF16),
+            jax.ShapeDtypeStruct((width, ff), BF16),
+            jax.ShapeDtypeStruct((ff, width), BF16),
+        ],
+        in_specs=[
+            whole((width, rows)),
+            whole((ff, rows)),
+            side((rows, narrow)),
+            side((rows, narrow)),
+            side((rows, wide)),
+            whole((share, width)),
+            whole((share, width)),
+        ],
+        out_specs=[
+            whole((share, width)),
+            whole((share, width)),
+            side((width, narrow)),
+            side((width, narrow)),
+            side((ff, wide)),
+        ],
+        compiler_params=pltpu.CompilerParams(vmem_limit_bytes=60 * 1024 * 1024),
+        cost_estimate=pl.CostEstimate(
+            flops=flops // 2, bytes_accessed=6 * width * ff, transcendentals=0
+        ),
+    )(rows_xt, hidden_t, gpg, gpu, rows_c, mixed, grad_tokens)
+    return (mixed, grad_tokens, grad_gate[None], grad_up[None], grad_down[None])
 
 
 def capacity_of(tok_rows, top_count, groups):

time: 81.7 us -> 70.1 us (0.86)
  matrix products: 16.7 us -> 0 us
  Pallas kernels: 60 us -> 68.5 us
  local copies, waits for them, and re-layouts: 4.17 us -> 0 us
    dot_general x3 -> x0, matrix products: 16.7 us -> none  [local_fused(): lax.dot_general(a, b, (((0,), (0,)), ((), ())), preferred_element_type=F32)]
    pallas_call x0 -> x1, Pallas kernels: none -> 11.4 us  [local_fused(): pl.pallas_call(weights_kernel, grid=(steps,), out_shape=[jax.ShapeDtypeSt...]
    unnamed x16 -> x0, local copies, waits for them, and re-layouts: 4.17 us -> none
    pallas_call x1, Pallas kernels: 60 us -> 57.1 us  [local_fused(): pl.pallas_call(functools.partial(layer_kernel, groups, quarter, tile), ou...]
where the time goes in v2:
time: 70.1 us; the launch traced here: 69.2 us
  Pallas kernels  68.5 us (98%)
    pallas_call x1, Pallas kernels, local_fused(): pl.pallas_call(functools.partial(layer_kernel, groups, quarter, tile), ou...  57.1 us
    pallas_call x1, Pallas kernels, local_fused(): pl.pallas_call(weights_kernel, grid=(steps,), out_shape=[jax.ShapeDtypeSt...  11.4 us

profile of v2, /device:TPU:0, one launch (start us, length us, event | category | flops | bytes accessed | tf_op | source)
XLA Modules:
  0.0 69.2 jit_solution(11286600857816221307)
XLA Ops:
  0.6 57.1 %shard_map.110 = (bf16[2304,256]{1,0:T(8,128)(2,1)}, bf16[256,2304]{1,0:T(8,128)(2,1)}, bf16[1536,256]{1,0:T(8,128)(2,1)}, bf16[256,1536]{1,0:T(8,128)(2,1)}, bf...) custom-call(bf16[128,2304]{1,0:T(8,128)(2,1)} %tok.1, s32[2,128]{1,0:T(2,128)} %bitcast.11, ...), custom_call_target="tpu_custom_call" | custom-call | flops 10871635968 | bytes 21233664 | tf_op jit(solution)/shard_map/pallas_call | solution.py:392
  57.7 11.4 %shard_map.111 = (bf16[32,2304]{1,0:T(8,128)(2,1)}, bf16[32,2304]{1,0:T(8,128)(2,1)}, bf16[2304,1536]{1,0:T(8,128)(2,1)}, bf16[2304,1536]{1,0:T(8,128)(2,1)}, bf16[1536,2304]{1,0:T(8,128)(2,1)}) custom-call(bf16[2304,256]{1,0:T(8,128)(2,1)} %get-tuple-element.17.rows_xt, bf16[1536,256]{1,0:T(8,128)(2,1)} %get-tuple-element.18.hidden_t, ...), custom_call_target="tpu_custom_call" | custom-call | flops 5435817984 | bytes 21233664 | tf_op jit(solution)/shard_map/pallas_call | solution.py:447

commit v3 on v2

--- a/solution.py
+++ b/solution.py
@@ -360,9 +360,15 @@
         mixed_out[...] = mixed[...]
         gtok_out[...] = gtok[...]
 
-    grad_gate[...] = nn(rows_xt[...], gpg[...]).astype(BF16)
-    grad_up[...] = nn(rows_xt[...], gpu[...]).astype(BF16)
-    grad_down[...] = nn(hidden_t[...], rows_c[...]).astype(BF16)
+    for left, right, out in (
+        (rows_xt, gpg, grad_gate),
+        (rows_xt, gpu, grad_up),
+        (hidden_t, rows_c, grad_down),
+    ):
+        piece = 768 if left.shape[0] % 768 == 0 else 256
+        for m in range(0, left.shape[0], piece):
+            at = slice(m, m + piece)
+            out[at, :] = nn(left[at, :], right[...]).astype(BF16)
 
 
 def fits(tokens, capacity, shares, width, ff):

time: 70.1 us -> 70.2 us (level)
  no operation moved by 1% of the time
where the time goes in v3:
time: 70.2 us; the launch traced here: 69.2 us
  Pallas kernels  68.5 us (98%)
    pallas_call x1, Pallas kernels, local_fused(): pl.pallas_call(functools.partial(layer_kernel, groups, quarter, tile), ou...  57.1 us
    pallas_call x1, Pallas kernels, local_fused(): pl.pallas_call(weights_kernel, grid=(steps,), out_shape=[jax.ShapeDtypeSt...  11.4 us

profile of v3, /device:TPU:0, one launch (start us, length us, event | category | flops | bytes accessed | tf_op | source)
XLA Modules:
  0.0 69.2 jit_solution(6870807786235653420)
XLA Ops:
  0.6 57.1 %shard_map.110 = (bf16[2304,256]{1,0:T(8,128)(2,1)}, bf16[256,2304]{1,0:T(8,128)(2,1)}, bf16[1536,256]{1,0:T(8,128)(2,1)}, bf16[256,1536]{1,0:T(8,128)(2,1)}, bf...) custom-call(bf16[128,2304]{1,0:T(8,128)(2,1)} %tok.1, s32[2,128]{1,0:T(2,128)} %bitcast.11, ...), custom_call_target="tpu_custom_call" | custom-call | flops 10871635968 | bytes 21233664 | tf_op jit(solution)/shard_map/pallas_call | solution.py:398
  57.7 11.4 %shard_map.111 = (bf16[32,2304]{1,0:T(8,128)(2,1)}, bf16[32,2304]{1,0:T(8,128)(2,1)}, bf16[2304,1536]{1,0:T(8,128)(2,1)}, bf16[2304,1536]{1,0:T(8,128)(2,1)}, bf16[1536,2304]{1,0:T(8,128)(2,1)}) custom-call(bf16[2304,256]{1,0:T(8,128)(2,1)} %get-tuple-element.17.rows_xt, bf16[1536,256]{1,0:T(8,128)(2,1)} %get-tuple-element.18.hidden_t, ...), custom_call_target="tpu_custom_call" | custom-call | flops 5435817984 | bytes 21233664 | tf_op jit(solution)/shard_map/pallas_call | solution.py:453
